TPU v7x, 32 devices: a whole 2x2x4 slice. The times are simulated.
32 devices in a mesh: row: 2 (over x), col: 16 (over z, y, core).
Axes of the slice: x: 2, y: 2, z: 4, core: 2. Of those that a mesh axis runs over, the one named last changes fastest.
Arguments:
- sigma_owned: float32 [2048, 2048], P('row', 'col'), may hold values from -1 to 45, as said below
- diag_b: float32 [512, 512], replicated, may hold values from -1 to 45
- panel_b: float32 [2048, 512], P(('row', 'col')), may hold values from -0.5 to 0.5
- pattern_b: int32 [16, 4], replicated, may hold values from 0 to 1, as said below
- diag_a: float32 [512, 512], replicated, may hold values from -1 to 45
- panel_a: float32 [2048, 512], P(('row', 'col')), may hold values from -0.5 to 0.5
- pattern_a: int32 [16, 4], replicated, may hold values from 0 to 1, as said below
- coupling: float32 [512, 512], P('col'), may hold values from -0.25 to 0.25
Outputs:
- sigma_sb: float32 [2048, 512], P(('row', 'col'))
- sigma_bb: float32 [512, 512], replicated
- sigma_sa: float32 [2048, 512], P(('row', 'col'))
- sigma_ba: float32 [512, 512], replicated
- sigma_aa: float32 [512, 512], replicated
Inputs may be any that keep to these rules, and one draw needn't show every extreme that they name: `sigma_owned`: the columns of a symmetric matrix, in the owner order of the first step. `pattern_b`: every block row holds at least one nonzero block. `pattern_a`: every block row holds at least one nonzero block.
All inputs are finite; a program needn't handle non-finite values.
Results may differ from a plain program's by a relative error of at most 0.000071.
Values sent between devices are 32-bit elements; how exact they have to be, the bound alone decides.
A program may use at most 64 MiB of HBM per device.

v0:
```python
import jax
import jax.numpy as jnp
from jax import lax
from jax.sharding import PartitionSpec as P

BLOCK = 128


def highest(left, right):
    return jnp.dot(left, right, precision=lax.Precision.HIGHEST, preferred_element_type=jnp.float32)


def inner(left, right):
    return lax.dot_general(
        left,
        right,
        (((0,), (0,)), ((), ())),
        precision=lax.Precision.HIGHEST,
        preferred_element_type=jnp.float32,
    )


def masked(panel, pattern):
    row_count = panel.shape[0]
    location = lax.axis_index("row") * lax.axis_size("col") + lax.axis_index("col")
    row_ids = location * row_count + lax.iota(jnp.int32, row_count)
    block_ids = row_ids // BLOCK
    selector = (block_ids[:, None] == lax.iota(jnp.int32, pattern.shape[0])[None, :]).astype(
        jnp.float32
    )
    row_mask = highest(selector, pattern.astype(jnp.float32))
    return panel * jnp.repeat(row_mask, BLOCK, axis=1)


def propagate(sigma_local, panel):
    readers = lax.all_gather(panel, "row", axis=0, tiled=True)
    result = lax.psum_scatter(highest(sigma_local, readers), "col", scatter_dimension=0, tiled=True)
    return result


def shards(sigma_owned, diag_b, panel_b, pattern_b, diag_a, panel_a, pattern_a, coupling):
    masked_b = masked(panel_b, pattern_b)
    masked_a = masked(panel_a, pattern_a)
    image_b = propagate(sigma_owned, masked_b)
    coupled = lax.all_gather(coupling, "col", axis=0, tiled=True)
    update_bb = lax.psum(inner(masked_b, image_b), ("row", "col"))
    cross_term = lax.psum(inner(image_b, masked_a), ("row", "col"))
    image_as = propagate(sigma_owned, masked_a) - highest(image_b, coupled)
    update_aa = lax.psum(inner(masked_a, image_as), ("row", "col"))
    sigma_bb = diag_b + update_bb
    image_ab = highest(sigma_bb, coupled) - cross_term
    sigma_aa = diag_a + update_aa + inner(coupled, image_ab)
    return (-image_b, sigma_bb, -image_as, -image_ab, sigma_aa)


def solution(mesh):
    in_specs = (
        P("row", "col"),
        P(),
        P(("row", "col"), None),
        P(),
        P(),
        P(("row", "col"), None),
        P(),
        P("col", None),
    )
    out_specs = (P(("row", "col"), None), P(), P(("row", "col"), None), P(), P())
    return jax.shard_map(shards, mesh=mesh, in_specs=in_specs, out_specs=out_specs, check_vma=False)
```

profile of v0, /device:TPU:0, one launch (start us, length us, event | category | flops | bytes accessed | tf_op | source)
XLA Modules:
  0.0 340.3 jit_solution(4691948546559415259)
XLA Ops:
  7.2 0.0 all-gather.2.cloned.1.call-start
  7.2 0.7 all-gather.2.cloned.1.call-update
  7.9 0.0 reduce-scatter.9.cloned.1.call-start
  8.0 0.9 fusion.1
  8.9 0.1 broadcast_in_dim.5
  9.0 0.9 bitcast_multiply_fusion
  9.9 7.1 %all_gather.10 = f32[128,512]{1,0:T(8,128)S(1)} all-gather(f32[64,512]{1,0:T(8,128)S(1)} %bitcast_multiply_fusion), channel_id=1, replica_groups=mesh['row'=2,'col'=16] {'row'}, dimensions={0}, use_global_device_ids=true | all-gather | bytes 393216 | tf_op jit(solution)/shard_map/all_gather | solution.py:36
  17.0 1.8 convolution_bitcast_fusion
  18.9 1.8 copy.29
  20.7 0.0 reduce-scatter.9.cloned.1.call-update
  20.7 0.0 reduce-scatter.7.cloned.1.call-start
  20.8 0.6 copy-done.9
  21.4 0.2 fusion.2
  21.6 0.1 broadcast_in_dim.4
  21.8 5.6 %all_gather.9 = f32[128,512]{1,0:T(8,128)S(1)} all-gather(f32[64,512]{1,0:T(8,128)S(1)} %bitcast_multiply_fusion.1), channel_id=1, replica_groups=mesh['row'=2,'col'=16] {'row'}, dimensions={0}, use_global_device_ids=true | all-gather | bytes 393216 | tf_op jit(solution)/shard_map/all_gather | solution.py:36
  27.4 1.8 convolution_bitcast_fusion.1
  29.3 1.9 copy.27
  31.1 0.2 all-reduce.3.cloned.1.call-start
  31.4 19.5 %all-gather.2.cloned.1.call-done = f32[512,512]{1,0:T(8,128)} async-done(((f32[32,512]{1,0:T(8,128)}), f32[512,512]{1,0:T(8,128)}) %all-gather.2.cloned.1.call-update) | async-done | bytes 1048592 | tf_op jit(solution)/shard_map/all_gather | solution.py:45
  50.9 64.2 %reduce-scatter.9.cloned.1.call-done = f32[64,512]{1,0:T(8,128)} async-done(((f32[1024,512]{1,0:T(8,128)}), f32[64,512]{1,0:T(8,128)}) %reduce-scatter.9.cloned.1.call-update) | async-done | bytes 131088 | tf_op jit(solution)/shard_map/reduce_scatter | solution.py:37
  115.1 64.8 %reduce-scatter.7.cloned.1.call-done = f32[64,512]{1,0:T(8,128)} async-done(((f32[1024,512]{1,0:T(8,128)}), f32[64,512]{1,0:T(8,128)}) %reduce-scatter.7.cloned.1.call-update) | async-done | bytes 131088
  179.9 2.7 fusion.7
  182.6 2.0 fusion.11
  184.6 2.0 fusion.9
  186.6 2.0 fusion.10
  188.6 0.0 all-reduce.3.cloned.1.call-update
  188.7 0.1 copy.28
  188.8 0.8 copy.23
  189.6 136.9 %all-reduce.3.cloned.1.call-done = (f32[512,512]{1,0:T(8,128)}, f32[512,512]{1,0:T(8,128)}, f32[512,512]{1,0:T(8,128)}) async-done(((f32[512,512]{1,0:T(8,128)}, f32[512,512]{1,0:T(8,128)}, f32[512,512]{1,0:T(8,128)}), (f32[512,512]{1,0:T(8,128)}, f32[512,512]{1,0:T(8,128)}, f32[512,512]{1,0:T(8,128)})) %all-reduce.3.cloned.1.call-update) | async-done | bytes 3145744 | tf_op jit(solution)/shard_map/psum | solution.py:46
  326.5 1.5 add.43
  328.1 2.8 fusion.8
  330.9 2.9 fusion
  (23 shorter events, 0.1 us)
Async XLA Ops:
  7.2 9.9 %copy-start = (f32[1024,128]{1,0:T(8,128)S(1)}, f32[1024,128]{1,0:T(8,128)}, u32[]{:S(2)}) copy-start(f32[1024,128]{1,0:T(8,128)} %param.8) | copy-start | bytes 1572868
  7.2 43.7 %all-gather.2.cloned.1.call-start = ((), (), s32[]{:S(2)}) async-start(), calls=%async_computation.2 | async-start | bytes 1114112 | tf_op jit(solution)/shard_map/all_gather | solution.py:45
  7.9 107.2 %reduce-scatter.9.cloned.1.call-start = ((), (), s32[]{:S(2)}) async-start(), calls=%async_computation.4 | async-start | bytes 2228224 | tf_op jit(solution)/shard_map/reduce_scatter | solution.py:37
  20.7 0.7 copy-start.9
  20.7 1.0 copy-start.8
  20.7 159.2 %reduce-scatter.7.cloned.1.call-start = ((), (), s32[]{:S(2)}) async-start(), calls=%async_computation.3 | async-start | bytes 2228224
  31.1 295.3 %all-reduce.3.cloned.1.call-start = ((), (), s32[]{:S(2)}) async-start(), calls=%async_computation.5 | async-start | bytes 6291456 | tf_op jit(solution)/shard_map/psum | solution.py:46
  179.9 4.7 %copy-start.3 = (f32[64,512]{1,0:T(8,128)S(1)}, f32[64,512]{1,0:T(8,128)}, u32[]{:S(2)}) copy-start(f32[64,512]{1,0:T(8,128)} %reduce-scatter.7.cloned.1.call-done) | copy-start | bytes 393220
  188.6 137.8 %copy-start.4 = (f32[512,512]{1,0:T(8,128)S(1)}, f32[512,512]{1,0:T(8,128)}, u32[]{:S(2)}) copy-start(f32[512,512]{1,0:T(8,128)} %param.9) | copy-start | bytes 3145732
  188.8 139.2 %copy-start.1 = (f32[512,512]{1,0:T(8,128)S(1)}, f32[512,512]{1,0:T(8,128)}, u32[]{:S(2)}) copy-start(f32[512,512]{1,0:T(8,128)} %all-gather.2.cloned.1.call-done) | copy-start | bytes 3145732
  326.5 1.6 copy-start.7
  328.0 2.9 copy-start.2
  328.0 2.9 copy-start.5
  328.0 2.9 copy-start.6
Sparse Core Ops, SparseCore 0:
  10.2 40.6 all-gather.1
  54.6 60.4 reduce-scatter.8
  119.3 60.5 reduce-scatter.6
  188.8 137.6 all-reduce.2
where the time goes:
time: 341 us; the launch traced here: 340 us
  waiting for transfers between devices  286 us (84%)
  matrix products  19.2 us (6%)
  between operations  13.9 us (4%)
  blocking collectives  12.7 us (4%)
  local copies, waits for them, and re-layouts  5.49 us (2%)
    psum x1, waiting for transfers between devices, shards(): update_bb = lax.psum(inner(masked_b, image_b), ('row', 'col'))  137 us
    unnamed x5, waiting for transfers between devices  65.6 us
    reduce_scatter x1, waiting for transfers between devices, propagate(): lax.psum_scatter(highest(sigma_local, readers), 'col', scatter_dimension=...  64.2 us
    all_gather x1, waiting for transfers between devices, shards(): coupled = lax.all_gather(coupling, 'col', axis=0, tiled=True)  19.5 us
    all_gather x2, blocking collectives, propagate(): readers = lax.all_gather(panel, 'row', axis=0, tiled=True)  12.7 us
    dot_general x6, matrix products, highest(): jnp.dot(left, right, precision=lax.Precision.HIGHEST, preferred_element_t...  10.3 us
    dot_general x4, matrix products, inner(): lax.dot_general(left, right, (((0,), (0,)), ((), ())), precision=lax.Prec...  8.87 us
  transfers between devices with their start and end apart: 4, of which 4 were waited for; matrix products, arithmetic and copies ran while one was open for 3% of the time, Pallas kernels for 0%

commit v1 on v0

v1 whole, which is shorter than its diff:
```python
import functools

import jax
import jax.numpy as jnp
from jax import lax
from jax.experimental import pallas as pl
from jax.experimental.pallas import tpu as pltpu
from jax.sharding import PartitionSpec as P

BLOCK = 128
LANES = 128
MESH = pl.DeviceIdType.MESH


def split(x):
    high = x.astype(jnp.bfloat16)
    low = (x - high.astype(jnp.float32)).astype(jnp.bfloat16)
    return high, low


def product(left, right):
    (lh, ll), (rh, rl) = left, right
    dot = functools.partial(jnp.dot, preferred_element_type=jnp.float32)
    return dot(lh, rh) + (dot(lh, rl) + dot(ll, rh))


def masked(panel, pattern):
    rows = panel.shape[0]
    location = lax.axis_index("row") * lax.axis_size("col") + lax.axis_index("col")
    own = lax.dynamic_slice_in_dim(pattern, location * rows // BLOCK, 1, axis=0)
    return jnp.where(jnp.repeat(own, BLOCK, axis=1) == 1, panel, 0.0)


def kernel(
    R, C,
    sigma_ref, pb_ref, pa_ref, db_ref, da_ref, cp_ref,
    sb_ref, bb_ref, sa_ref, ba_ref, aa_ref,
    m, cpl, g1, g2, st, t, trecv, img, arecv, part, core_in, piece, peer_in,
    cw_send, cw_recv, ccw_send, ccw_recv, sib_send, sib_recv,
    t_send, t_recv, a_send, a_recv, c_send, c_recv, p_send, p_recv,
):
    G, W = pb_ref.shape
    NB = W // LANES
    H = C // NB
    Y = H // 2
    n = C // 2
    ncw, nccw = n // 2, (n - 1) // 2
    r = lax.axis_index("row")
    c = lax.axis_index("col")
    chip, core = c // 2, c % 2
    i_me, h = c // H, c % H
    y_me = h // 2
    sibling = c + 1 - 2 * core

    def chip_at(k):
        k = (k + n) % n
        return 2 * k + (k // (n // 2)) * (2 * (n - 1 - k) + 1 - 2 * k)

    k_me = chip // 2 + (chip % 2) * (n - 1 - 2 * (chip // 2))
    right = chip_at(k_me + 1) * 2 + core
    left = chip_at(k_me - 1) * 2 + core

    barrier = pltpu.get_barrier_semaphore()
    count = 0
    for d in range(1, C):
        pl.semaphore_signal(barrier, inc=1, device_id=(r, (c + d) % C), device_id_type=MESH)
        count += 1
    for dr in range(1, R):
        for dy in range(Y):
            peer = i_me * H + ((y_me + dy) % Y) * 2 + core
            pl.semaphore_signal(barrier, inc=1, device_id=((r + dr) % R, peer), device_id_type=MESH)
            count += 1

    slots = [
        lambda q: m.at[0, q],
        lambda q: m.at[1, q],
        lambda q: cpl.at[q],
        lambda q: g1.at[:, q],
        lambda q: g2.at[q],
    ]
    m[0, c] = pb_ref[...]
    m[1, c] = pa_ref[...]
    cpl[c] = cp_ref[...]
    pl.semaphore_wait(barrier, count)

    unsent = []

    def push(src, dst, send, recv, device):
        copy = pltpu.make_async_remote_copy(
            src_ref=src, dst_ref=dst, send_sem=send, recv_sem=recv,
            device_id=device, device_id_type=MESH,
        )
        copy.start()
        unsent.append(copy)
        return copy

    arrivals = {}

    def to_sibling(p, k, q):
        arrivals["s", p, k] = push(slots[p](q), slots[p](q), sib_send.at[p, k], sib_recv.at[p, k], (r, sibling))

    def go_right(p, s, q):
        arrivals["r", p, s] = push(slots[p](q), slots[p](q), cw_send.at[p, s], cw_recv.at[p, s], (r, right))

    def go_left(p, s, q):
        arrivals["l", p, s] = push(slots[p](q), slots[p](q), ccw_send.at[p, s], ccw_recv.at[p, s], (r, left))

    def begin(p):
        go_right(p, 0, c)
        if nccw:
            go_left(p, 0, c)
        to_sibling(p, 0, c)

    def tick(p, s):
        if s < ncw:
            q = chip_at(k_me - (s + 1)) * 2 + core
            arrivals["r", p, s].wait_recv()
            if s + 1 < ncw:
                go_right(p, s + 1, q)
            to_sibling(p, 1 + s, q)
        if s < nccw:
            q = chip_at(k_me + (s + 1)) * 2 + core
            arrivals["l", p, s].wait_recv()
            if s + 1 < nccw:
                go_left(p, s + 1, q)
            to_sibling(p, 1 + ncw + s, q)

    def settle(p):
        for k in range(n):
            arrivals["s", p, k].wait_recv()

    def multiply(p):
        rows = m.shape[1] * G
        t[p] = product((st[0], st[1]), split(m[p].reshape(rows, W)))
        for d in range(1, R):
            to = (r + d) % R
            arrivals["t", p, d] = push(
                t.at[p, pl.ds(pl.multiple_of(to * G, G), G)], trecv.at[p, d - 1],
                t_send.at[p, d - 1], t_recv.at[p, d - 1], (to, c),
            )

    def spread(p):
        total = t[p, pl.ds(pl.multiple_of(r * G, G), G)]
        for d in range(1, R):
            arrivals["t", p, d].wait_recv()
            total += trecv[p, d - 1]
        for b in range(NB):
            img[p, b] = total[:, b * LANES:(b + 1) * LANES]
        for d in range(1, NB):
            to = (i_me + d) % NB
            arrivals["a", p, d] = push(
                img.at[p, to], arecv.at[p, d - 1],
                a_send.at[p, d - 1], a_recv.at[p, d - 1], (r, to * H + h),
            )
        return total

    def image_block(p):
        blocks = [img[p, i_me]]
        for d in range(1, NB):
            arrivals["a", p, d].wait_recv()
            blocks.append(arecv[p, d - 1])
        return split(jnp.concatenate(blocks, axis=0).T)

    def gram(k, block, p):
        rows = [m[p, ((i_me + NB - d) % NB) * H + h] for d in range(NB)]
        part[k] = product(block, split(jnp.concatenate(rows, axis=0))).reshape(part.shape[1:])
        arrivals["c", k] = push(
            part.at[k, :, 1 - core], core_in.at[k], c_send.at[k], c_recv.at[k], (r, sibling)
        )

    def pair_sum(k):
        arrivals["c", k].wait_recv()
        piece[k] = part[k, :, core] + core_in[k]
        for d in range(1, R * Y):
            dr, dy = d // Y, d % Y
            y_to = (y_me + dy) % Y
            arrivals["p", k, d] = push(
                piece.at[k, y_to], peer_in.at[k, d - 1], p_send.at[k, d - 1], p_recv.at[k, d - 1],
                ((r + dr) % R, i_me * H + y_to * 2 + core),
            )

    def layer_sum(k):
        total = piece[k, y_me]
        for d in range(1, R * Y):
            arrivals["p", k, d].wait_recv()
            total += peer_in[k, d - 1]
        return total

    ticks = ncw
    half = ticks // 2
    begin(0)
    transposed = split(sigma_ref[...].T)
    st[0] = transposed[0]
    st[1] = transposed[1]
    for s in range(half):
        tick(0, s)
    begin(1)
    for s in range(half, ticks):
        tick(0, s)
        tick(1, s - half)
    settle(0)
    multiply(0)
    begin(2)
    for s in range(ticks - half, ticks):
        tick(1, s)
    image_b = spread(0)
    sb_ref[...] = -image_b
    settle(1)
    multiply(1)
    block = image_block(0)
    gram(0, block, 0)
    gram(1, block, 1)
    image_a = spread(1)
    pair_sum(0)
    pair_sum(1)
    for s in range(half):
        tick(2, s)
    gram(2, image_block(1), 1)
    g1[0, c] = layer_sum(0)
    g1[1, c] = layer_sum(1)
    begin(3)
    pair_sum(2)
    for s in range(half, ticks):
        tick(2, s)
    tick(3, 0)
    g2[c] = layer_sum(2)
    begin(4)
    settle(2)
    for s in range(1, ticks):
        tick(3, s)
        tick(4, s - 1)
    settle(3)
    tick(4, ticks - 1)
    coupling = cpl[...].reshape(W, W)
    coupled = split(coupling)
    sa_ref[...] = product(split(image_b), coupled) - image_a
    bb = db_ref[...] + g1[0].reshape(W, W)
    bb_ref[...] = bb
    cross = g1[1].reshape(W, W)
    ab = product(split(bb), coupled) - cross
    ba_ref[...] = -ab
    tail = product(split(coupling.T), split(ab)) - product(split(cross.T), coupled)
    settle(4)
    aa_ref[...] = da_ref[...] + tail + g2[...].reshape(W, W)
    for copy in unsent:
        copy.wait_send()


def shards(sigma_owned, diag_b, panel_b, pattern_b, diag_a, panel_a, pattern_a, coupling):
    R, C = lax.axis_size("row"), lax.axis_size("col")
    G, W = panel_b.shape
    NB = W // LANES
    Y = C // NB // 2
    n = C // 2
    pc = W // C
    f32, bf16 = jnp.float32, jnp.bfloat16
    shape = lambda *dims: jax.ShapeDtypeStruct(dims, f32)
    dma = pltpu.SemaphoreType.DMA
    vmem = pl.BlockSpec(memory_space=pltpu.VMEM)
    return pl.pallas_call(
        functools.partial(kernel, R, C),
        out_shape=(shape(G, W), shape(W, W), shape(G, W), shape(W, W), shape(W, W)),
        in_specs=[vmem] * 6,
        out_specs=(vmem,) * 5,
        scratch_shapes=[
            pltpu.VMEM((2, C, G, W), f32),
            pltpu.VMEM((C, coupling.shape[0], W), f32),
            pltpu.VMEM((2, C, pc, W), f32),
            pltpu.VMEM((C, pc, W), f32),
            pltpu.VMEM((2, R * G, C * G), bf16),
            pltpu.VMEM((2, R * G, W), f32),
            pltpu.VMEM((2, max(R - 1, 1), G, W), f32),
            pltpu.VMEM((2, NB, G, LANES), f32),
            pltpu.VMEM((2, NB - 1, G, LANES), f32),
            pltpu.VMEM((3, Y, 2, pc, W), f32),
            pltpu.VMEM((3, Y, pc, W), f32),
            pltpu.VMEM((3, Y, pc, W), f32),
            pltpu.VMEM((3, R * Y - 1, pc, W), f32),
            dma((5, n // 2)), dma((5, n // 2)),
            dma((5, (n - 1) // 2)), dma((5, (n - 1) // 2)),
            dma((5, n)), dma((5, n)),
            dma((2, R - 1)), dma((2, R - 1)),
            dma((2, NB - 1)), dma((2, NB - 1)),
            dma((3,)), dma((3,)),
            dma((3, R * Y - 1)), dma((3, R * Y - 1)),
        ],
        compiler_params=pltpu.CompilerParams(
            collective_id=0, has_side_effects=True, vmem_limit_bytes=48 * 1024 * 1024
        ),
    )(sigma_owned, masked(panel_b, pattern_b), masked(panel_a, pattern_a), diag_b, diag_a, coupling)


def solution(mesh):
    in_specs = (
        P("row", "col"),
        P(),
        P(("row", "col"), None),
        P(),
        P(),
        P(("row", "col"), None),
        P(),
        P("col", None),
    )
    out_specs = (P(("row", "col"), None), P(), P(("row", "col"), None), P(), P())
    return jax.shard_map(shards, mesh=mesh, in_specs=in_specs, out_specs=out_specs, check_vma=False)
```

time: 341 us -> 95.2 us (0.28)
  waiting for transfers between devices: 286 us -> 0 us
  Pallas kernels: 0 us -> 85.8 us
  matrix products: 19.2 us -> 0 us
  between operations: 13.9 us -> 0.71 us
  blocking collectives: 12.7 us -> 0 us
    psum x1 -> x0, waiting for transfers between devices: 137 us -> none  [shards(): update_bb = lax.psum(inner(masked_b, image_b), ('row', 'col'))]
    pallas_call x0 -> x1, Pallas kernels: none -> 85.8 us  [shards(): pl.pallas_call(functools.partial(kernel, R, C), out_shape=(shape(G, W), s...]
    unnamed x5 -> x0, waiting for transfers between devices: 65.6 us -> none
    reduce_scatter x1 -> x0, waiting for transfers between devices: 64.2 us -> none  [propagate(): lax.psum_scatter(highest(sigma_local, readers), 'col', scatter_dimension=...]
    all_gather x1 -> x0, waiting for transfers between devices: 19.5 us -> none  [shards(): coupled = lax.all_gather(coupling, 'col', axis=0, tiled=True)]
    dot_general x10 -> x0, matrix products: 19.2 us -> none  [the longest x6 10.3 us: highest(): jnp.dot(left, right, precision=lax.Precision.HIGHEST, preferred_element_t...]
    all_gather x2 -> x0, blocking collectives: 12.7 us -> none  [propagate(): readers = lax.all_gather(panel, 'row', axis=0, tiled=True)]
  transfers between devices with their start and end apart: 4 -> 0, of which waited for: 4 -> 0; matrix products, arithmetic and copies ran while one was open for 3% -> 0% of each run, Pallas kernels for 0% -> 0%
where the time goes in v1:
time: 95.2 us; the launch traced here: 95 us
  Pallas kernels  85.8 us (90%)
  local copies, waits for them, and re-layouts  5.6 us (6%)
  other arithmetic  2.85 us (3%)
    pallas_call x1, Pallas kernels, shards(): pl.pallas_call(functools.partial(kernel, R, C), out_shape=(shape(G, W), s...  85.8 us
    unnamed x11, local copies, waits for them, and re-layouts  5.45 us

profile of v1, /device:TPU:0, one launch (start us, length us, event | category | flops | bytes accessed | tf_op | source)
XLA Modules:
  0.0 95.0 jit_solution(447225556878505245)
XLA Ops:
  0.6 0.0 copy-start.1
  0.7 1.0 %fusion = (pred[4]{0:T(512)(128)(4,1)S(1)}, pred[4]{0:T(512)(128)(4,1)S(1)}) fusion(s32[16,4]{0,1:T(4,128)} %param.11, s32[]{:T(128)S(6)} %select_n.18, s32[16,4]{0,1:T(4,128)} %param.14), kind=kLoop, calls=%fused_computation.4 | loop fusion | flops 8 | bytes 44 | tf_op jit(solution)/shard_map/eq | solution.py:31
  1.6 0.1 broadcast_bitcast_fusion.1
  1.7 0.1 broadcast_bitcast_fusion
  1.8 0.9 broadcast_select_fusion.pa_ref
  2.7 0.0 copy-start.2
  2.7 0.9 %broadcast_select_fusion.1.pb_ref = f32[64,512]{1,0:T(8,128)S(1)} fusion(f32[64,512]{1,0:T(8,128)} %param.10, pred[512]{0:T(512)(128)(4,1)S(1)} %broadcast_bitcast_fusion.1), kind=kLoop, calls=%fused_computation.1 | loop fusion | flops 32768 | bytes 262656 | tf_op jit(solution)/shard_map/jit(_where)/select_n | solution.py:31
  3.7 0.0 copy-done.1
  3.7 0.0 copy-done.2
  3.7 0.0 copy-start
  3.7 1.2 %copy-done = f32[512,512]{1,0:T(8,128)S(1)} copy-done((f32[512,512]{1,0:T(8,128)S(1)}, f32[512,512]{1,0:T(8,128)}, u32[]{:S(2)}) %copy-start) | copy-done | bytes 1048600
  4.9 85.8 %shard_map.119 = (f32[64,512]{1,0:T(8,128)S(1)}, f32[512,512]{1,0:T(8,128)S(1)}, f32[64,512]{1,0:T(8,128)S(1)}, f32[512,512]{1,0:T(8,128)S(1)}, f32[512,512]{1,0:T(8,128)S(1)}) custom-call(f32[1024,128]{1,0:T(8,128)S(1)} %copy-done.1, f32[64,512]{1,0:T(8,128)S(1)} %broadcast_select_fusion.1.pb_ref, f32[64,512]{1,0:T(8,128)S(1)} %broadcast_select_fusion.pa_ref, ...), custom_call_target="tpu_custom_call" | custom-call | tf_op jit(solution)/shard_map/pallas_call | solution.py:260
  90.8 0.7 copy.18
  91.4 1.0 %copy.19 = f32[512,512]{1,0:T(8,128)} copy(f32[512,512]{1,0:T(8,128)S(1)} %get-tuple-element.13) | data formatting | bytes 2097152
  92.4 0.7 copy.20
  93.1 1.0 %copy.21 = f32[512,512]{1,0:T(8,128)} copy(f32[512,512]{1,0:T(8,128)S(1)} %get-tuple-element.15) | data formatting | bytes 2097152
  94.0 1.0 %copy.22 = f32[512,512]{1,0:T(8,128)} copy(f32[512,512]{1,0:T(8,128)S(1)} %get-tuple-element.16) | data formatting | bytes 2097152
Async XLA Ops:
  0.6 3.0 %copy-start.1 = (f32[1024,128]{1,0:T(8,128)S(1)}, f32[1024,128]{1,0:T(8,128)}, u32[]{:S(2)}) copy-start(f32[1024,128]{1,0:T(8,128)} %sigma_ref.1) | copy-start | bytes 1572868
  2.7 1.0 %copy-start.2 = (f32[32,512]{1,0:T(8,128)S(1)}, f32[32,512]{1,0:T(8,128)}, u32[]{:S(2)}) copy-start(f32[32,512]{1,0:T(8,128)} %cp_ref.1) | copy-start | bytes 196612
  3.7 1.2 %copy-start = (f32[512,512]{1,0:T(8,128)S(1)}, f32[512,512]{1,0:T(8,128)}, u32[]{:S(2)}) copy-start(f32[512,512]{1,0:T(8,128)} %db_ref.1) | copy-start | bytes 3145732

commit v2 on v1

v2 whole, which is shorter than its diff:
```python
import functools

import jax
import jax.numpy as jnp
from jax import lax
from jax.experimental import pallas as pl
from jax.experimental.pallas import tpu as pltpu
from jax.sharding import PartitionSpec as P

BLOCK = 128
LANES = 128
MESH = pl.DeviceIdType.MESH


def split(x):
    high = x.astype(jnp.bfloat16)
    low = (x - high.astype(jnp.float32)).astype(jnp.bfloat16)
    return high, low


def product(left, right):
    (lh, ll), (rh, rl) = left, right
    dot = functools.partial(jnp.dot, preferred_element_type=jnp.float32)
    return dot(lh, rh) + (dot(lh, rl) + dot(ll, rh))


def kernel(
    R, C, X,
    sigma_ref, pb_ref, pa_ref, patb_ref, pata_ref, db_ref, da_ref, cp_ref,
    sb_ref, bb_ref, sa_ref, ba_ref, aa_ref,
    m, cpl, g1, g2, st, t, trecv, img, arecv, part, core_in, piece, peer_in,
    z_send, z_recv, y_send, y_recv, x_send, x_recv, sib_send, sib_recv,
    t_send, t_recv, a_send, a_recv, c_send, c_recv, p_send, p_recv,
):
    G, W = pb_ref.shape
    NB = W // LANES
    H = C // NB
    Y = H // 2
    n = C // 2
    r = lax.axis_index("row")
    c = lax.axis_index("col")
    core = c % 2
    i_me, h = c // H, c % H
    y_me = h // 2
    sibling = c + 1 - 2 * core

    barrier = pltpu.get_barrier_semaphore()
    count = 0
    for d in range(1, C):
        pl.semaphore_signal(barrier, inc=1, device_id=(r, (c + d) % C), device_id_type=MESH)
        count += 1
    for dr in range(1, R):
        for dy in range(Y):
            peer = i_me * H + ((y_me + dy) % Y) * 2 + core
            pl.semaphore_signal(barrier, inc=1, device_id=((r + dr) % R, peer), device_id_type=MESH)
            count += 1

    top, low = slice(0, G // 2), slice(G // 2, G)
    slots = [
        lambda q, x: m.at[0, q, top],
        lambda q, x: m.at[0, q, low],
        lambda q, x: m.at[1, q, top],
        lambda q, x: m.at[1, q, low],
        lambda q, x: cpl.at[q, x],
        lambda q, x: g1.at[:, q, x],
        lambda q, x: g2.at[q, x],
    ]
    B, A, CP, G1, G2 = (0, 1), (2, 3), 4, 5, 6
    x_me = r % X
    block_row = (r * C + c) * G // BLOCK
    for p, panel, pattern in ((0, pb_ref, patb_ref), (1, pa_ref, pata_ref)):
        for b in range(W // BLOCK):
            columns = slice(b * BLOCK, (b + 1) * BLOCK)
            m[p, c, :, columns] = jnp.where(pattern[block_row, b] == 1, panel[:, columns], 0.0)
    own_rows = cp_ref[...].reshape(cpl.shape[1:])
    for x in range(X):
        cpl[c, x] = own_rows[x]
    pl.semaphore_wait(barrier, count)

    unsent = []

    def push(src, dst, send, recv, device):
        copy = pltpu.make_async_remote_copy(
            src_ref=src, dst_ref=dst, send_sem=send, recv_sem=recv,
            device_id=device, device_id_type=MESH,
        )
        copy.start()
        unsent.append(copy)
        return copy

    arrivals = {}

    def slot_of(p, d, e, f=0):
        q = ((i_me + NB - d) % NB) * H + ((y_me + Y - e) % Y) * 2 + core
        return slots[p](q, (r + X - f) % X)

    def to_sibling(p, d, e, f=0):
        k = (f * Y + e) * NB + d
        ref = slot_of(p, d, e, f)
        arrivals["s", p, k] = push(ref, ref, sib_send.at[p, k], sib_recv.at[p, k], (r, sibling))

    def to_rows(p, d, e):
        if p < CP:
            return
        k = e * NB + d
        ref = slot_of(p, d, e)
        for f in range(1, X):
            arrivals["x", p, k, f] = push(
                ref, ref, x_send.at[p - CP, f - 1, k], x_recv.at[p - CP, f - 1, k], ((r + f) % R, c)
            )

    def to_group(p, d):
        ref = slot_of(p, d, 0)
        for e in range(1, Y):
            arrivals["y", p, e, d] = push(
                ref, ref, y_send.at[p, e - 1, d], y_recv.at[p, e - 1, d],
                (r, i_me * H + ((y_me + e) % Y) * 2 + core),
            )

    def begin(p):
        ref = slot_of(p, 0, 0)
        for d in range(1, NB):
            arrivals["z", p, d] = push(
                ref, ref, z_send.at[p, d - 1], z_recv.at[p, d - 1], (r, ((i_me + d) % NB) * H + h)
            )
        to_group(p, 0)
        to_rows(p, 0, 0)
        to_sibling(p, 0, 0)

    def forward_z(p):
        for d in range(1, NB):
            arrivals["z", p, d].wait_recv()
            to_group(p, d)
            to_rows(p, d, 0)
            to_sibling(p, d, 0)

    def forward_y(p):
        for d in range(NB):
            for e in range(1, Y):
                arrivals["y", p, e, d].wait_recv()
                to_rows(p, d, e)
                to_sibling(p, d, e)

    def forward_x(p):
        for f in range(1, X):
            for e in range(Y):
                for d in range(NB):
                    arrivals["x", p, e * NB + d, f].wait_recv()
                    to_sibling(p, d, e, f)

    def settle(p):
        for k in range(n * (X if p >= CP else 1)):
            arrivals["s", p, k].wait_recv()

    def multiply(p):
        rows = m.shape[1] * G
        t[p] = product((st[0], st[1]), split(m[p].reshape(rows, W)))
        for d in range(1, R):
            to = (r + d) % R
            arrivals["t", p, d] = push(
                t.at[p, pl.ds(pl.multiple_of(to * G, G), G)], trecv.at[p, d - 1],
                t_send.at[p, d - 1], t_recv.at[p, d - 1], (to, c),
            )

    def spread(p):
        total = t[p, pl.ds(pl.multiple_of(r * G, G), G)]
        for d in range(1, R):
            arrivals["t", p, d].wait_recv()
            total += trecv[p, d - 1]
        for b in range(NB):
            img[p, b] = total[:, b * LANES:(b + 1) * LANES]
        for d in range(1, NB):
            to = (i_me + d) % NB
            arrivals["a", p, d] = push(
                img.at[p, to], arecv.at[p, d - 1],
                a_send.at[p, d - 1], a_recv.at[p, d - 1], (r, to * H + h),
            )
        return total

    def image_block(p):
        blocks = [img[p, i_me]]
        for d in range(1, NB):
            arrivals["a", p, d].wait_recv()
            blocks.append(arecv[p, d - 1])
        return split(jnp.concatenate(blocks, axis=0).T)

    def gram(k, block, p):
        rows = [m[p, ((i_me + NB - d) % NB) * H + h] for d in range(NB)]
        part[k] = product(block, split(jnp.concatenate(rows, axis=0))).reshape(part.shape[1:])
        arrivals["c", k] = push(
            part.at[k, :, 1 - core], core_in.at[k], c_send.at[k], c_recv.at[k], (r, sibling)
        )

    def pair_sum(k):
        arrivals["c", k].wait_recv()
        piece[k] = (part[k, :, core] + core_in[k]).reshape(piece.shape[1:])
        for d in range(1, R * Y):
            dr, dy = d // Y, d % Y
            y_to = (y_me + dy) % Y
            r_to = (r + dr) % R
            arrivals["p", k, d] = push(
                piece.at[k, y_to, r_to % X], peer_in.at[k, d - 1], p_send.at[k, d - 1], p_recv.at[k, d - 1],
                (r_to, i_me * H + y_to * 2 + core),
            )

    def layer_sum(k):
        total = piece[k, y_me, x_me]
        for d in range(1, R * Y):
            arrivals["p", k, d].wait_recv()
            total += peer_in[k, d - 1]
        return total

    begin(0)
    begin(1)
    transposed = split(sigma_ref[...].T)
    st[0] = transposed[0]
    st[1] = transposed[1]
    forward_z(0)
    begin(2)
    forward_z(1)
    begin(3)
    forward_y(0)
    forward_y(1)
    forward_z(2)
    settle(0)
    settle(1)
    multiply(0)
    forward_z(3)
    forward_y(2)
    image_b = spread(0)
    sb_ref[...] = -image_b
    forward_y(3)
    settle(2)
    settle(3)
    multiply(1)
    begin(CP)
    block = image_block(0)
    gram(0, block, 0)
    gram(1, block, 1)
    pair_sum(0)
    pair_sum(1)
    image_a = spread(1)
    forward_z(CP)
    g1[0, c, x_me] = layer_sum(0)
    g1[1, c, x_me] = layer_sum(1)
    begin(G1)
    gram(2, image_block(1), 1)
    forward_y(CP)
    pair_sum(2)
    forward_z(G1)
    g2[c, x_me] = layer_sum(2)
    begin(G2)
    forward_x(CP)
    forward_y(G1)
    settle(CP)
    coupling = cpl[...].reshape(W, W)
    coupled = split(coupling)
    sa_ref[...] = product(split(image_b), coupled) - image_a
    forward_z(G2)
    forward_x(G1)
    forward_y(G2)
    settle(G1)
    bb = db_ref[...] + g1[0].reshape(W, W)
    bb_ref[...] = bb
    cross = g1[1].reshape(W, W)
    ab = product(split(bb), coupled) - cross
    ba_ref[...] = -ab
    forward_x(G2)
    tail = product(split(coupling.T), split(ab)) - product(split(cross.T), coupled)
    settle(G2)
    aa_ref[...] = da_ref[...] + tail + g2[...].reshape(W, W)
    for copy in unsent:
        copy.wait_send()


def shards(sigma_owned, diag_b, panel_b, pattern_b, diag_a, panel_a, pattern_a, coupling):
    R, C = lax.axis_size("row"), lax.axis_size("col")
    G, W = panel_b.shape
    NB = W // LANES
    Y = C // NB // 2
    n = C // 2
    pc = W // C
    X = R if pc % (8 * R) == 0 else 1
    px = pc // X
    f32, bf16 = jnp.float32, jnp.bfloat16
    shape = lambda *dims: jax.ShapeDtypeStruct(dims, f32)
    dma = pltpu.SemaphoreType.DMA
    vmem = pl.BlockSpec(memory_space=pltpu.VMEM)
    smem = pl.BlockSpec(memory_space=pltpu.SMEM)
    return pl.pallas_call(
        functools.partial(kernel, R, C, X),
        out_shape=(shape(G, W), shape(W, W), shape(G, W), shape(W, W), shape(W, W)),
        in_specs=[vmem] * 3 + [smem] * 2 + [vmem] * 3,
        out_specs=(vmem,) * 5,
        scratch_shapes=[
            pltpu.VMEM((2, C, G, W), f32),
            pltpu.VMEM((C, X, px, W), f32),
            pltpu.VMEM((2, C, X, px, W), f32),
            pltpu.VMEM((C, X, px, W), f32),
            pltpu.VMEM((2, R * G, C * G), bf16),
            pltpu.VMEM((2, R * G, W), f32),
            pltpu.VMEM((2, max(R - 1, 1), G, W), f32),
            pltpu.VMEM((2, NB, G, LANES), f32),
            pltpu.VMEM((2, NB - 1, G, LANES), f32),
            pltpu.VMEM((3, Y, 2, pc, W), f32),
            pltpu.VMEM((3, Y, pc, W), f32),
            pltpu.VMEM((3, Y, X, px, W), f32),
            pltpu.VMEM((3, R * Y - 1, px, W), f32),
            dma((7, NB - 1)), dma((7, NB - 1)),
            dma((7, Y - 1, NB)), dma((7, Y - 1, NB)),
            dma((3, max(X - 1, 1), n)), dma((3, max(X - 1, 1), n)),
            dma((7, n * X)), dma((7, n * X)),
            dma((2, R - 1)), dma((2, R - 1)),
            dma((2, NB - 1)), dma((2, NB - 1)),
            dma((3,)), dma((3,)),
            dma((3, R * Y - 1)), dma((3, R * Y - 1)),
        ],
        compiler_params=pltpu.CompilerParams(
            collective_id=0, has_side_effects=True, vmem_limit_bytes=48 * 1024 * 1024
        ),
    )(sigma_owned, panel_b, panel_a, pattern_b, pattern_a, diag_b, diag_a, coupling)


def solution(mesh):
    in_specs = (
        P("row", "col"),
        P(),
        P(("row", "col"), None),
        P(),
        P(),
        P(("row", "col"), None),
        P(),
        P("col", None),
    )
    out_specs = (P(("row", "col"), None), P(), P(("row", "col"), None), P(), P())
    return jax.shard_map(shards, mesh=mesh, in_specs=in_specs, out_specs=out_specs, check_vma=False)
```

time: 95.2 us -> 87.4 us (0.918)
  Pallas kernels: 85.8 us -> 76.1 us
  local copies, waits for them, and re-layouts: 5.6 us -> 9.98 us
  other arithmetic: 2.85 us -> 0 us
    pallas_call x1, Pallas kernels: 85.8 us -> 76.1 us  [shards(): pl.pallas_call(functools.partial(kernel, R, C, X), out_shape=(shape(G, W)...]
    unnamed x11 -> x19, local copies, waits for them, and re-layouts: 5.45 us -> 9.98 us
    select_n x2 -> x0, other arithmetic: 1.88 us -> none  [masked(): return jnp.where(jnp.repeat(own, BLOCK, axis=1) == 1, panel, 0.0)]
    eq x1 -> x0, other arithmetic: 0.97 us -> none  [masked(): return jnp.where(jnp.repeat(own, BLOCK, axis=1) == 1, panel, 0.0)]
where the time goes in v2:
time: 87.4 us; the launch traced here: 86.7 us
  Pallas kernels  76.1 us (87%)
  local copies, waits for them, and re-layouts  9.98 us (11%)
    pallas_call x1, Pallas kernels, shards(): pl.pallas_call(functools.partial(kernel, R, C, X), out_shape=(shape(G, W)...  76.1 us
    unnamed x19, local copies, waits for them, and re-layouts  9.98 us

profile of v2, /device:TPU:0, one launch (start us, length us, event | category | flops | bytes accessed | tf_op | source)
XLA Modules:
  0.0 86.7 jit_solution(5410106053856443667)
XLA Ops:
  0.6 0.0 copy-start.5
  0.6 0.8 copy.13.patb_ref
  1.4 0.0 copy-done.5
  1.4 0.1 copy.14.pata_ref
  1.5 0.0 copy-start
  1.5 1.2 %copy-done = f32[512,512]{1,0:T(8,128)S(1)} copy-done((f32[512,512]{1,0:T(8,128)S(1)}, f32[512,512]{1,0:T(8,128)}, u32[]{:S(2)}) %copy-start) | copy-done | bytes 1048600
  2.7 0.0 copy-start.1
  2.7 1.0 %copy-done.1 = f32[1024,128]{1,0:T(8,128)S(1)} copy-done((f32[1024,128]{1,0:T(8,128)S(1)}, f32[1024,128]{1,0:T(8,128)}, u32[]{:S(2)}) %copy-start.1) | copy-done | bytes 524312
  3.8 0.0 copy-start.2
  3.8 0.9 %copy-done.2 = f32[64,512]{1,0:T(8,128)S(1)} copy-done((f32[64,512]{1,0:T(8,128)S(1)}, f32[64,512]{1,0:T(8,128)}, u32[]{:S(2)}) %copy-start.2) | copy-done | bytes 131096
  4.7 0.0 copy-start.3
  4.7 0.9 %copy-done.3 = f32[64,512]{1,0:T(8,128)S(1)} copy-done((f32[64,512]{1,0:T(8,128)S(1)}, f32[64,512]{1,0:T(8,128)}, u32[]{:S(2)}) %copy-start.3) | copy-done | bytes 131096
  5.6 0.0 copy-start.4
  5.6 0.8 copy-done.4
  6.4 76.1 %shard_map.119 = (f32[64,512]{1,0:T(8,128)S(1)}, f32[512,512]{1,0:T(8,128)S(1)}, f32[64,512]{1,0:T(8,128)S(1)}, f32[512,512]{1,0:T(8,128)S(1)}, f32[512,512]{1,0:T(8,128)S(1)}) custom-call(f32[1024,128]{1,0:T(8,128)S(1)} %copy-done.1, f32[64,512]{1,0:T(8,128)S(1)} %copy-done.2, f32[64,512]{1,0:T(8,128)S(1)} %copy-done.3, s32[16,4]{1,0:T(8,128)S(1)} %copy.13.patb_ref, ...), custom_call_target="tpu_custom_call" | custom-call | tf_op jit(solution)/shard_map/pallas_call | solution.py:290
  82.5 0.7 copy.20
  83.2 1.0 %copy.21 = f32[512,512]{1,0:T(8,128)} copy(f32[512,512]{1,0:T(8,128)S(1)} %get-tuple-element.11) | data formatting | bytes 2097152
  84.1 0.7 copy.22
  84.8 1.0 %copy.23 = f32[512,512]{1,0:T(8,128)} copy(f32[512,512]{1,0:T(8,128)S(1)} %get-tuple-element.13) | data formatting | bytes 2097152
  85.8 1.0 %copy.24 = f32[512,512]{1,0:T(8,128)} copy(f32[512,512]{1,0:T(8,128)S(1)} %get-tuple-element.14) | data formatting | bytes 2097152
Async XLA Ops:
  0.6 0.8 copy-start.5
  1.5 1.2 %copy-start = (f32[512,512]{1,0:T(8,128)S(1)}, f32[512,512]{1,0:T(8,128)}, u32[]{:S(2)}) copy-start(f32[512,512]{1,0:T(8,128)} %db_ref.1) | copy-start | bytes 3145732
  2.7 1.0 %copy-start.1 = (f32[1024,128]{1,0:T(8,128)S(1)}, f32[1024,128]{1,0:T(8,128)}, u32[]{:S(2)}) copy-start(f32[1024,128]{1,0:T(8,128)} %sigma_ref.1) | copy-start | bytes 1572868
  3.8 0.9 %copy-start.2 = (f32[64,512]{1,0:T(8,128)S(1)}, f32[64,512]{1,0:T(8,128)}, u32[]{:S(2)}) copy-start(f32[64,512]{1,0:T(8,128)} %pb_ref.1) | copy-start | bytes 393220
  4.7 0.9 %copy-start.3 = (f32[64,512]{1,0:T(8,128)S(1)}, f32[64,512]{1,0:T(8,128)}, u32[]{:S(2)}) copy-start(f32[64,512]{1,0:T(8,128)} %pa_ref.1) | copy-start | bytes 393220
  5.6 0.8 copy-start.4
